TPU v7x, 32 devices: a whole 2x2x4 slice. The times are simulated.
32 devices in a mesh: grp: 2 (over x), op: 16 (over z, y, core).
Axes of the slice: x: 2, y: 2, z: 4, core: 2. Of those that a mesh axis runs over, the one named last changes fastest.
Arguments:
- wavefunction: bfloat16 [4, 2048, 256], P('grp', 'op'), parts along dimension 0, may hold values from -6 to 6
- left_ops: bfloat16 [1024, 256, 256], P(('grp', 'op')), parts along dimension 0, may hold values from -0.375 to 0.375
- right_ops: bfloat16 [1024, 256, 256], P(('grp', 'op')), parts along dimension 0, may hold values from -0.0546875 to 0.0546875
- left_index: int32 [3072], P(('grp', 'op')), parts along dimension 0, may hold values from 0 to 31
- right_index: int32 [3072], P(('grp', 'op')), parts along dimension 0, may hold values from 0 to 31
- source_block: int32 [3072], P(('grp', 'op')), parts along dimension 0, may hold values from 0 to 7
- target_block: int32 [3072], P(('grp', 'op')), parts along dimension 0, may hold values from 0 to 7
- live_count: int32 [32], P(('grp', 'op')), parts along dimension 0, may hold values from 1 to 96, as said below
Outputs:
- sigma: float32 [4, 2048, 256], P('grp', 'op'), parts along dimension 0
There are 2 independent parts, one for each index of `grp`. A program takes and returns all parts, laid end to end along the dimension named above; each array names one. Nothing has to cross between parts.
Inputs may be any that keep to these rules, and one draw needn't show every extreme that they name: `live_count`: the live terms of an operator group occupy its first slots; in every draw one group has all 96 slots live.
All inputs are finite; a program needn't handle non-finite values.
Results may differ from a plain program's by a relative error of at most 0.003.
Values may be sent and summed in bfloat16 or wider, within the bound.
A program may use at most 128 MiB of HBM per device.

v0:
```python
import math

import jax
import jax.numpy as jnp
from jax import lax
from jax.sharding import PartitionSpec as P


def sweep(lefts_table, rights_table, term_lists, first_slot, end_slot, blocks, summed, batch):
    left_pick, right_pick, source_pick, target_pick = term_lists
    nblocks = blocks.shape[1]

    def advance(turn, running):
        offset = turn * batch
        lefts = jnp.take(lefts_table, lax.dynamic_slice_in_dim(left_pick, offset, batch), axis=0)
        rights = jnp.take(rights_table, lax.dynamic_slice_in_dim(right_pick, offset, batch), axis=0)
        picked = jnp.take(blocks, lax.dynamic_slice_in_dim(source_pick, offset, batch), axis=1)
        targets = lax.dynamic_slice_in_dim(target_pick, offset, batch)
        left_part = jnp.einsum(
            "kij,vkjm->kvim", lefts, picked, preferred_element_type=jnp.float32
        ).astype(jnp.bfloat16)
        term_part = jnp.einsum(
            "kvim,kmn->kvin", left_part, rights, preferred_element_type=jnp.float32
        )
        slot_ids = offset + jnp.arange(batch, dtype=jnp.int32)
        active = ((slot_ids >= first_slot) & (slot_ids < end_slot)).astype(jnp.float32)
        term_part = term_part * active[:, None, None, None]
        return running + jax.ops.segment_sum(term_part, targets, num_segments=nblocks)

    return lax.fori_loop(first_slot // batch, (end_slot + batch - 1) // batch, advance, summed)


def per_device(
    wavefunction,
    left_ops,
    right_ops,
    left_index,
    right_index,
    source_block,
    target_block,
    live_count,
):
    width = left_ops.shape[1]
    gathered = lax.all_gather(wavefunction, "op", axis=1, tiled=True)
    nblocks = gathered.shape[1] // width
    blocks = gathered.reshape(2, nblocks, width, width)
    batch = math.gcd(left_index.shape[0], 16)
    summed = jnp.zeros((nblocks, 2, width, width), jnp.float32)
    own_lists = (left_index, right_index, source_block, target_block)
    own_count = live_count[0]
    zero_slot = jnp.int32(0)
    summed = sweep(left_ops, right_ops, own_lists, zero_slot, own_count, blocks, summed, batch)
    partial_sigma = summed.transpose(1, 0, 2, 3).reshape(2, nblocks * width, width)
    return lax.psum_scatter(partial_sigma, "op", scatter_dimension=1, tiled=True)


def solution(mesh):
    in_specs = (
        P("grp", "op", None),
        P(("grp", "op"), None, None),
        P(("grp", "op"), None, None),
        P(("grp", "op")),
        P(("grp", "op")),
        P(("grp", "op")),
        P(("grp", "op")),
        P(("grp", "op")),
    )
    out_specs = P("grp", "op", None)
    return jax.shard_map(
        per_device, mesh=mesh, in_specs=in_specs, out_specs=out_specs, check_vma=False
    )
```

profile of v0, /device:TPU:0, one launch (start us, length us, event | category | flops | bytes accessed | tf_op | source)
XLA Modules:
  0.0 372.3 jit_solution(330836940873034221)
XLA Ops:
  6.5 0.0 copy-start.4
  6.5 0.0 copy-start.1
  6.5 0.0 copy-start.3
  6.5 0.0 copy-start.2
  6.5 0.0 all-gather.2.cloned.1.call-start
  6.6 0.7 all-gather.2.cloned.1.call-update
  7.3 0.0 reduce-scatter.2.cloned.1.call-start
  8.0 45.7 %all-gather.2.cloned.1.call-done = bf16[2,2048,256]{2,1,0:T(8,128)(2,1)} async-done(((bf16[2,128,256]{2,1,0:T(8,128)(2,1)}), bf16[2,2048,256]{2,1,0:T(8,128)(2,1)}) %all-gather.2.cloned.1.call-update) | async-done | bytes 2097168 | tf_op jit(solution)/shard_map/all_gather | solution.py:44
  53.7 0.0 copy-start
  53.7 2.4 broadcast.43
  56.1 0.0 copy-done.4
  56.1 0.0 copy-done.1
  56.1 0.0 copy-done.3
  56.1 0.0 copy-done.2
  56.1 0.0 copy-done
  56.1 39.0 %while.10 = (s32[]{:T(128)}, f32[8,2,256,256]{3,2,1,0:T(8,128)}, s32[]{:T(128)}, s32[96]{0:T(128)S(1)}, s32[96]{0:T(128)S(1)}, /*index=5*/bf16[2,8,256,256]{3,2,...) while((s32[]{:T(128)}, f32[8,2,256,256]{3,2,1,0:T(8,128)}, ...), condition=%wide.region_2.4_spmd, body=%wide.region_0.3_spmd.sunk | while | flops 2157972736 | bytes 58733936 | solution.py:30
  56.1 0.1 dynamic_slice.19
  56.2 0.7 compare_and_fusion.5
  56.9 0.1 compare_and_fusion.6
  57.1 4.2 %gather_fusion.2 = bf16[16,256,256]{2,1,0:T(8,128)(2,1)} fusion(bf16[32,256,256]{2,1,0:T(8,128)(2,1)} %get-tuple-element.215, s32[1024]{0:T(1024)S(1)} %pad_clamp_fusion.8), kind=kCustom, calls=%fused_computation.clone.clone.1 | custom fusion | bytes 4194368 | tf_op jit(solution)/shard_map/while/body/jit(_take)/gather | solution.py:15
  61.2 4.2 %gather_fusion.1 = bf16[16,256,256]{2,1,0:T(8,128)(2,1)} fusion(bf16[32,256,256]{2,1,0:T(8,128)(2,1)} %get-tuple-element.217, s32[1024]{0:T(1024)S(1)} %pad_clamp_fusion.7), kind=kCustom, calls=%fused_computation.1.clone.clone.1 | custom fusion | bytes 4194368 | tf_op jit(solution)/shard_map/while/body/jit(_take)/gather | solution.py:16
  65.4 2.8 gather_fusion
  68.2 9.2 %broadcast_multiply_fusion.2 = f32[16,2,256,256]{3,2,1,0:T(8,128)} fusion(f32[16]{0:T(128)S(1)} %get-tuple-element.171, bf16[16,2,256,256]{3,2,1,0:T(8,128)(2,1)} %gather_fusion, pred[16]{0:T(512)(128)(4,1)S(1)} %get-tuple-element.173, bf16[16,256,256]{2,1,0:T(8,128)(2,1)} %gather_fusion.1, bf16[16,256,256]{2,1,0:T(8,128)(2,1)} %gather_fusion.2, ...), kind=kOutput, calls=%fused_computation.9.clone.1 | convolution fusion | flops 2155872256 | bytes 16777328 | tf_op jit(solution)/shard_map/while/body/kvim,kmn->kvin/dot_general | solution.py:22
  77.5 17.7 %scatter_fusion = f32[8,2,256,256]{3,2,1,0:T(8,128)} fusion(f32[8,2,256,256]{3,2,1,0:T(8,128)} %get-tuple-element.194, s32[16]{0:T(128)S(1)} %dynamic_slice.19, f32[16,2,256,256]{3,2,1,0:T(8,128)} %broadcast_multiply_fusion.2), kind=kCustom, calls=%fused_computation.3.clone.1 | custom fusion | flops 2097152 | bytes 25165888 | tf_op jit(solution)/shard_map/while/body/scatter-add | solution.py:28
  95.1 4.5 %copy.9 = f32[2,8,256,256]{3,2,1,0:T(8,128)} copy(f32[2,8,256,256]{3,2,0,1:T(8,128)} %bitcast.36) | data formatting | bytes 8388608 | tf_op jit(solution)/shard_map/transpose | solution.py:53
  99.6 0.0 reduce-scatter.2.cloned.1.call-update
  99.7 265.9 %reduce-scatter.2.cloned.1.call-done = f32[2,128,256]{2,1,0:T(8,128)} async-done(((f32[2,2048,256]{2,1,0:T(8,128)}), f32[2,128,256]{2,1,0:T(8,128)}) %reduce-scatter.2.cloned.1.call-update) | async-done | bytes 262160 | tf_op jit(solution)/shard_map/reduce_scatter | solution.py:54
  (3 shorter events, 0.0 us)
Async XLA Ops:
  6.5 49.6 %copy-start.4 = (s32[96]{0:T(128)S(1)}, s32[96]{0:T(128)}, u32[]{:S(2)}) copy-start(s32[96]{0:T(128)} %param.18) | copy-start | bytes 1156
  6.5 49.6 %copy-start.1 = (s32[96]{0:T(128)S(1)}, s32[96]{0:T(128)}, u32[]{:S(2)}) copy-start(s32[96]{0:T(128)} %param.17) | copy-start | bytes 1156
  6.5 49.6 %copy-start.3 = (s32[96]{0:T(128)S(1)}, s32[96]{0:T(128)}, u32[]{:S(2)}) copy-start(s32[96]{0:T(128)} %param.16) | copy-start | bytes 1156
  6.5 49.6 %copy-start.2 = (s32[96]{0:T(128)S(1)}, s32[96]{0:T(128)}, u32[]{:S(2)}) copy-start(s32[96]{0:T(128)} %param.15) | copy-start | bytes 1156
  6.5 47.2 %all-gather.2.cloned.1.call-start = ((), (), s32[]{:S(2)}) async-start(), calls=%async_computation.1 | async-start | bytes 2228224 | tf_op jit(solution)/shard_map/all_gather | solution.py:44
  7.3 358.2 %reduce-scatter.2.cloned.1.call-start = ((), (), s32[]{:S(2)}) async-start(), calls=%async_computation.2 | async-start | bytes 4456448 | tf_op jit(solution)/shard_map/reduce_scatter | solution.py:54
  53.7 2.4 copy-start
Sparse Core Ops, SparseCore 0:
  9.6 44.1 all-gather.1
  99.8 265.6 reduce-scatter.1
where the time goes:
time: 374 us; the launch traced here: 372 us
  waiting for transfers between devices  312 us (83%)
  other arithmetic  18.5 us (5%)
  local copies, waits for them, and re-layouts  18.1 us (5%)
  between operations  14.1 us (4%)
  matrix products  9.24 us (2%)
    reduce_scatter x1, waiting for transfers between devices, per_device(): lax.psum_scatter(partial_sigma, 'op', scatter_dimension=1, tiled=True)  266 us
    all_gather x1, waiting for transfers between devices, per_device(): gathered = lax.all_gather(wavefunction, 'op', axis=1, tiled=True)  45.7 us
    scatter-add x1, other arithmetic, advance(): jax.ops.segment_sum(term_part, targets, num_segments=nblocks)  17.7 us
    dot_general x1, matrix products, advance(): jnp.einsum('kvim,kmn->kvin', left_part, rights, preferred_element_type=jn...  9.24 us
  transfers between devices with their start and end apart: 2, of which 2 were waited for; matrix products, arithmetic and copies ran while one was open for 0% of the time, Pallas kernels for 0%

commit v1 on v0

v1 whole, which is shorter than its diff:
```python
import functools

import jax
import jax.numpy as jnp
from jax import lax
from jax.experimental import pallas as pl
from jax.experimental.pallas import tpu as pltpu
from jax.sharding import PartitionSpec as P

MESH = pl.DeviceIdType.MESH
UNROLL = 2
SEGMENTS = 6


def plan_terms(left_index, right_index, source_block, target_block, live_count, nblocks):
    slots = left_index.shape[0]
    ids = jnp.arange(slots, dtype=jnp.int32)
    target = jnp.where(ids < live_count[0], target_block, nblocks)
    key = target * slots + ids
    rank = jnp.sum((key[None, :] < key[:, None]).astype(jnp.int32), axis=1)
    place = (rank[None, :] == ids[:, None]).astype(jnp.int32)
    rows = jnp.stack([left_index, right_index, source_block, target])
    rows = jnp.sum(rows[:, None, :] * place[None], axis=2)
    before = jnp.concatenate([jnp.full((1,), -1, jnp.int32), rows[3, :-1]])
    keep = (rows[3] == before).astype(jnp.int32)
    ends = jnp.sum((target[None, :] <= ids[:, None]).astype(jnp.int32), axis=1)
    any_term = jnp.sum((target[None, :] == ids[:, None]).astype(jnp.int32), axis=1) > 0
    return jnp.concatenate([rows[:3], jnp.stack([keep, ends, any_term.astype(jnp.int32)])])


def kernel(far, near, plan, wave, left_hbm, right_hbm, out,
           lefts, rights, psi0, psi1, hist, ended, send_c, recv_c, send_y, recv_y, send_z, recv_z,
           ops_sem, zsem, ysem, csem):
    psi = (psi0, psi1)
    rows = wave.shape[1]
    width = wave.shape[2]
    slots = plan.shape[1]
    me = lax.axis_index("op")
    c = lax.rem(me, 2)
    y = lax.rem(me // 2, near)
    z = me // (2 * near)

    def index_of(a, b, core):
        return (a * near + b) * 2 + core

    def place_of(idx):
        row = idx * rows
        return row // width, pl.ds(pl.multiple_of(lax.rem(row, width), rows), rows)

    def shift(at, by, size):
        return lax.rem(at + by + size, size)

    sibling = index_of(z, y, 1 - c)
    y_peer = [index_of(z, shift(y, d, near), c) for d in range(near)]
    z_peer = [index_of(shift(z, d, far), y, c) for d in range(far)]
    peers = [sibling] + y_peer[1:] + z_peer[1:]

    loads = [
        pltpu.make_async_copy(left_hbm, lefts, ops_sem.at[0]),
        pltpu.make_async_copy(right_hbm, rights, ops_sem.at[1]),
    ]
    for load in loads:
        load.start()
    barrier = pltpu.get_barrier_semaphore()
    for peer in peers:
        pl.semaphore_signal(barrier, inc=1, device_id={"op": peer}, device_id_type=MESH)
    for v in range(2):
        psi[v][place_of(me)] = wave[v]
    pl.semaphore_wait(barrier, len(peers))

    sent = []

    def remote(src, dst, sems, peer):
        return pltpu.make_async_remote_copy(
            src_ref=src, dst_ref=dst, send_sem=sems[0], recv_sem=sems[1],
            device_id={"op": peer}, device_id_type=MESH,
        )

    def send(src, dst, sems, peer):
        copy = remote(src, dst, sems, peer)
        copy.start()
        sent.append(copy)

    def sem_pair(array, *place):
        return array.at[(*place, 0)], array.at[(*place, 1)]

    def chunk(v, idx):
        return psi[v].at[place_of(idx)]

    def gather_copy(v, sems, idx, peer):
        send(chunk(v, idx), chunk(v, idx), sems, peer)

    def gather_wait(v, sems, idx, peer):
        remote(chunk(v, idx), chunk(v, idx), sems, peer).wait_recv()

    def source(dy, dz, core):
        return index_of(shift(z, -dz, far), shift(y, -dy, near), core)

    def spread(v, dz):
        idx = source(0, dz, c)
        for dy in range(1, near):
            gather_copy(v, sem_pair(ysem, 0, v, dy, dz), idx, y_peer[dy])
        gather_copy(v, sem_pair(csem, 0, v, 0, dz), idx, sibling)

    def gather_own(v):
        for dz in range(1, far):
            gather_copy(v, sem_pair(zsem, 0, v, dz), me, z_peer[dz])
        spread(v, 0)

    z_order = sorted(range(1, far), key=lambda d: min(d, far - d))

    def gather_far(v):
        for dz in z_order:
            gather_wait(v, sem_pair(zsem, 0, v, dz), source(0, dz, c), z_peer[dz])
            spread(v, dz)

    def gather_near(v):
        for dz in [0] + z_order:
            for dy in range(1, near):
                idx = source(dy, dz, c)
                gather_wait(v, sem_pair(ysem, 0, v, dy, dz), idx, y_peer[dy])
                gather_copy(v, sem_pair(csem, 0, v, dy, dz), idx, sibling)

    def gather_end(v):
        for dz in range(far):
            for dy in range(near):
                gather_wait(v, sem_pair(csem, 0, v, dy, dz), source(dy, dz, 1 - c), sibling)

    def terms(v, first, last):
        def body(i, carry):
            base = first + i * UNROLL
            parts = []
            for u in range(UNROLL):
                t = base + u
                block = psi[v][plan[2, t]]
                parts.append(
                    jnp.dot(lefts[plan[0, t]], block, preferred_element_type=jnp.float32)
                    .astype(jnp.bfloat16)
                )
            total = hist[base]
            for u in range(UNROLL):
                t = base + u
                total = total * plan[3, t].astype(jnp.float32) + jnp.dot(
                    parts[u], rights[plan[1, t]], preferred_element_type=jnp.float32
                )
                hist[t + 1] = total
            return carry

        lax.fori_loop(0, (last - first) // UNROLL, body, 0)

    def finish(v):
        for q in range(ended.shape[1]):
            ended[v, q] = hist[plan[4, q]] * plan[5, q].astype(jnp.float32)

    def partial(v, idx):
        return ended[(v, *place_of(idx))]

    f32 = jnp.float32
    bf16 = jnp.bfloat16

    def reduce_core(v):
        finish(v)
        for dy in list(range(1, near)) + [0]:
            for dz in z_order + [0]:
                a, b = shift(z, dz, far), shift(y, dy, near)
                send_c[v, dy, dz] = partial(v, index_of(a, b, 1 - c)).astype(bf16)
                send(send_c.at[v, dy, dz], recv_c.at[v, dy, dz], sem_pair(csem, 1, v, dy, dz), sibling)

    def core_sum(v, dy, dz):
        remote(send_c.at[v, dy, dz], recv_c.at[v, dy, dz], sem_pair(csem, 1, v, dy, dz), sibling).wait_recv()
        a, b = shift(z, dz, far), shift(y, dy, near)
        return partial(v, index_of(a, b, c)) + recv_c[v, dy, dz].astype(f32)

    def reduce_near(v):
        for dz in z_order + [0]:
            for dy in range(1, near):
                send_y[v, dy, dz] = core_sum(v, dy, dz).astype(bf16)
                send(send_y.at[v, dy, dz], recv_y.at[v, dy, dz], sem_pair(ysem, 1, v, dy, dz), y_peer[dy])

    def near_sum(v, dz):
        total = core_sum(v, 0, dz)
        for dy in range(1, near):
            remote(send_y.at[v, dy, dz], recv_y.at[v, dy, dz], sem_pair(ysem, 1, v, dy, dz), y_peer[dy]).wait_recv()
            total = total + recv_y[v, dy, dz].astype(f32)
        return total

    def reduce_far(v):
        for dz in z_order:
            send_z[v, dz] = near_sum(v, dz).astype(bf16)
            send(send_z.at[v, dz], recv_z.at[v, dz], sem_pair(zsem, 1, v, dz), z_peer[dz])
        out[v] = near_sum(v, 0)

    def reduce_end(v):
        total = out[v]
        for dz in z_order:
            remote(send_z.at[v, dz], recv_z.at[v, dz], sem_pair(zsem, 1, v, dz), z_peer[dz]).wait_recv()
            total = total + recv_z[v, dz].astype(f32)
        out[v] = total

    cuts = [slots * i // (SEGMENTS * UNROLL) * UNROLL for i in range(SEGMENTS)] + [slots]
    gather_own(0)
    hist[0] = jnp.zeros(hist.shape[1:], f32)
    gather_far(0)
    gather_own(1)
    gather_near(0)
    gather_end(0)
    for load in loads:
        load.wait()
    beside0 = {1: gather_far, 3: gather_near}
    for s in range(SEGMENTS):
        terms(0, cuts[s], cuts[s + 1])
        if s in beside0:
            beside0[s](1)
    gather_end(1)
    reduce_core(0)
    beside1 = {0: reduce_near, 3: reduce_far}
    for s in range(SEGMENTS):
        terms(1, cuts[s], cuts[s + 1])
        if s in beside1:
            beside1[s](0)
    reduce_core(1)
    reduce_near(1)
    reduce_far(1)
    reduce_end(0)
    reduce_end(1)
    for copy in sent:
        copy.wait_send()


def per_device(devices, wavefunction, left_ops, right_ops, left_index, right_index,
               source_block, target_block, live_count):
    pairs = devices // 2
    far = 1
    while far * far < pairs:
        far *= 2
    near = pairs // far
    vectors, rows, width = wavefunction.shape
    nblocks = devices * rows // width
    slots = left_index.shape[0]
    plan = plan_terms(left_index, right_index, source_block, target_block, live_count, nblocks)
    sems = pltpu.SemaphoreType.DMA
    bf16 = jnp.bfloat16
    f32 = jnp.float32
    spread = (2, near, far, rows, width)
    vmem = pl.BlockSpec(memory_space=pltpu.VMEM)
    hbm = pl.BlockSpec(memory_space=pl.ANY)
    return pl.pallas_call(
        functools.partial(kernel, far, near),
        out_shape=jax.ShapeDtypeStruct(wavefunction.shape, f32),
        in_specs=[pl.BlockSpec(memory_space=pltpu.SMEM), vmem, hbm, hbm],
        out_specs=vmem,
        scratch_shapes=[
            pltpu.VMEM(left_ops.shape, bf16),
            pltpu.VMEM(right_ops.shape, bf16),
            pltpu.VMEM((nblocks, width, width), bf16),
            pltpu.VMEM((nblocks, width, width), bf16),
            pltpu.VMEM((slots + 1, width, width), f32),
            pltpu.VMEM((2, nblocks, width, width), f32),
            pltpu.VMEM(spread, bf16),
            pltpu.VMEM(spread, bf16),
            pltpu.VMEM(spread, bf16),
            pltpu.VMEM(spread, bf16),
            pltpu.VMEM((2, far, rows, width), bf16),
            pltpu.VMEM((2, far, rows, width), bf16),
            sems((2,)),
            sems((2, 2, far, 2)),
            sems((2, 2, near, far, 2)),
            sems((2, 2, near, far, 2)),
        ],
        compiler_params=pltpu.CompilerParams(
            collective_id=0, has_side_effects=True, vmem_limit_bytes=56 * 1024 * 1024
        ),
        cost_estimate=pl.CostEstimate(
            flops=slots * vectors * 4 * width**3,
            bytes_accessed=4 * left_ops.size,
            transcendentals=0,
        ),
    )(plan, wavefunction, left_ops, right_ops)


def solution(mesh):
    rows = P("grp", "op", None)
    table = P(("grp", "op"), None, None)
    slots = P(("grp", "op"))
    return jax.shard_map(
        functools.partial(per_device, mesh.shape["op"]),
        mesh=mesh,
        in_specs=(rows, table, table, slots, slots, slots, slots, slots),
        out_specs=rows,
        check_vma=False,
    )
```

time: 374 us -> 73.2 us (0.20)
  waiting for transfers between devices: 312 us -> 0 us
  Pallas kernels: 0 us -> 68.3 us
  local copies, waits for them, and re-layouts: 18.1 us -> 1.68 us
  other arithmetic: 18.5 us -> 2.39 us
  between operations: 14.1 us -> 0.68 us
  matrix products: 9.24 us -> 0 us
    reduce_scatter x1 -> x0, waiting for transfers between devices: 266 us -> none  [per_device(): lax.psum_scatter(partial_sigma, 'op', scatter_dimension=1, tiled=True)]
    pallas_call x0 -> x1, Pallas kernels: none -> 68.3 us  [per_device(): pl.pallas_call(functools.partial(kernel, far, near), out_shape=jax.ShapeD...]
    all_gather x1 -> x0, waiting for transfers between devices: 45.7 us -> none  [per_device(): gathered = lax.all_gather(wavefunction, 'op', axis=1, tiled=True)]
    scatter-add x1 -> x0, other arithmetic: 17.7 us -> none  [advance(): jax.ops.segment_sum(term_part, targets, num_segments=nblocks)]
    gather x3 -> x0, local copies, waits for them, and re-layouts: 11.1 us -> none  [the longest x1 4.21 us: advance(): jnp.take(rights_table, lax.dynamic_slice_in_dim(right_pick, offset, batch...]
    dot_general x1 -> x0, matrix products: 9.24 us -> none  [advance(): jnp.einsum('kvim,kmn->kvin', left_part, rights, preferred_element_type=jn...]
    transpose x1 -> x0, local copies, waits for them, and re-layouts: 4.52 us -> none  [per_device(): summed.transpose(1, 0, 2, 3).reshape(2, nblocks * width, width)]
  transfers between devices with their start and end apart: 2 -> 0, of which waited for: 2 -> 0; matrix products, arithmetic and copies ran while one was open for 0% -> 0% of each run, Pallas kernels for 0% -> 0%
where the time goes in v1:
time: 73.2 us; the launch traced here: 73 us
  Pallas kernels  68.3 us (93%)
  other arithmetic  2.39 us (3%)
  local copies, waits for them, and re-layouts  1.68 us (2%)
    pallas_call x1, Pallas kernels, per_device(): pl.pallas_call(functools.partial(kernel, far, near), out_shape=jax.ShapeD...  68.3 us
    unnamed x1, local copies, waits for them, and re-layouts  1.67 us

profile of v1, /device:TPU:0, one launch (start us, length us, event | category | flops | bytes accessed | tf_op | source)
XLA Modules:
  0.0 73.0 jit_solution(11741414303144181780)
XLA Ops:
  0.7 0.7 iota_add_fusion
  1.3 0.2 convert_reduce_fusion.1
  1.5 0.7 pad_add_fusion.1
  2.2 0.1 multiply_reduce_fusion
  2.4 0.1 compare_convert_fusion.1
  2.4 0.6 pad_add_fusion.plan
  3.1 68.3 %shard_map.82 = f32[2,128,256]{2,1,0:T(8,128)} custom-call(s32[6,96]{1,0:T(8,128)} %pad_add_fusion.plan, bf16[2,128,256]{2,1,0:T(8,128)(2,1)} %wave.1, bf16[32,256,256]{2,1,0:T(8,128)(2,1)} %left_hbm.1, bf16[32,256,256]{2,1,0:T(8,128)(2,1)} %right_hbm.1), custom_call_target="tpu_custom_call" | custom-call | flops 12884901888 | bytes 8388608 | tf_op jit(solution)/shard_map/pallas_call | solution.py:247
  71.4 1.7 %copy.11 = f32[2,128,256]{2,1,0:T(8,128)} copy(f32[2,128,256]{2,1,0:T(8,128)} %shard_map.82) | data formatting | bytes 524288
  (3 shorter events, 0.0 us)

commit v2 on v1

--- a/solution.py
+++ b/solution.py
@@ -8,33 +8,48 @@
 from jax.sharding import PartitionSpec as P
 
 MESH = pl.DeviceIdType.MESH
-UNROLL = 2
+UNROLL = 16
 SEGMENTS = 6
 
 
-def plan_terms(left_index, right_index, source_block, target_block, live_count, nblocks):
-    slots = left_index.shape[0]
-    ids = jnp.arange(slots, dtype=jnp.int32)
-    target = jnp.where(ids < live_count[0], target_block, nblocks)
-    key = target * slots + ids
-    rank = jnp.sum((key[None, :] < key[:, None]).astype(jnp.int32), axis=1)
-    place = (rank[None, :] == ids[:, None]).astype(jnp.int32)
-    rows = jnp.stack([left_index, right_index, source_block, target])
-    rows = jnp.sum(rows[:, None, :] * place[None], axis=2)
-    before = jnp.concatenate([jnp.full((1,), -1, jnp.int32), rows[3, :-1]])
-    keep = (rows[3] == before).astype(jnp.int32)
-    ends = jnp.sum((target[None, :] <= ids[:, None]).astype(jnp.int32), axis=1)
-    any_term = jnp.sum((target[None, :] == ids[:, None]).astype(jnp.int32), axis=1) > 0
-    return jnp.concatenate([rows[:3], jnp.stack([keep, ends, any_term.astype(jnp.int32)])])
-
-
-def kernel(far, near, plan, wave, left_hbm, right_hbm, out,
-           lefts, rights, psi0, psi1, hist, ended, send_c, recv_c, send_y, recv_y, send_z, recv_z,
-           ops_sem, zsem, ysem, csem):
+def plan_terms(raw, live_count, nblocks):
+    lanes = raw.shape[1]
+    square = (lanes, lanes)
+    ids = lax.broadcasted_iota(jnp.int32, (1, lanes), 1)
+    across = lax.broadcasted_iota(jnp.int32, square, 1)
+    target = jnp.where(ids < live_count, raw[3:4], nblocks)
+
+    def down(row):
+        return jnp.broadcast_to(row, square).T
+
+    def count(mask):
+        return jnp.sum(mask.astype(jnp.int32), axis=0, keepdims=True)
+
+    key = target * lanes + ids
+    rank = down(count(down(key) < key))
+    target_down = down(target)
+
+    def sort(values, place):
+        return jnp.sum(jnp.where(place, values, 0), axis=0, keepdims=True)
+
+    place = rank == across
+    picked = [sort(down(raw[i : i + 1]), place) for i in range(3)]
+    ordered = sort(target_down + 1, place)
+    before = sort(target_down + 1, rank + 1 == across)
+    return picked + [
+        (ordered == before).astype(jnp.int32),
+        count(target_down <= across),
+        (count(target_down == across) > 0).astype(jnp.int32),
+    ]
+
+
+def kernel(far, near, live, left_index, right_index, source_block, target_block, wave, left_hbm, right_hbm, out,
+           raw, planned, plan, lefts, rights, psi0, psi1, hist, ended, send_c, recv_c, send_y, recv_y, send_z, recv_z,
+           ops_sem, plan_sem, zsem, ysem, csem):
     psi = (psi0, psi1)
     rows = wave.shape[1]
     width = wave.shape[2]
-    slots = plan.shape[1]
+    slots = left_index.shape[1]
     me = lax.axis_index("op")
     c = lax.rem(me, 2)
     y = lax.rem(me // 2, near)
@@ -102,15 +117,14 @@
             gather_copy(v, sem_pair(ysem, 0, v, dy, dz), idx, y_peer[dy])
         gather_copy(v, sem_pair(csem, 0, v, 0, dz), idx, sibling)
 
+    z_order = sorted(range(1, far), key=lambda d: min(d, far - d))
+
     def gather_own(v):
-        for dz in range(1, far):
+        for dz in z_order:
             gather_copy(v, sem_pair(zsem, 0, v, dz), me, z_peer[dz])
-        spread(v, 0)
-
-    z_order = sorted(range(1, far), key=lambda d: min(d, far - d))
-
-    def gather_far(v):
-        for dz in z_order:
+
+    def gather_far(v, order):
+        for dz in order:
             gather_wait(v, sem_pair(zsem, 0, v, dz), source(0, dz, c), z_peer[dz])
             spread(v, dz)
 
@@ -184,43 +198,64 @@
             total = total + recv_y[v, dy, dz].astype(f32)
         return total
 
-    def reduce_far(v):
-        for dz in z_order:
+    def reduce_far(v, order):
+        for dz in order:
             send_z[v, dz] = near_sum(v, dz).astype(bf16)
             send(send_z.at[v, dz], recv_z.at[v, dz], sem_pair(zsem, 1, v, dz), z_peer[dz])
-        out[v] = near_sum(v, 0)
 
     def reduce_end(v):
-        total = out[v]
+        total = near_sum(v, 0)
         for dz in z_order:
             remote(send_z.at[v, dz], recv_z.at[v, dz], sem_pair(zsem, 1, v, dz), z_peer[dz]).wait_recv()
             total = total + recv_z[v, dz].astype(f32)
         out[v] = total
 
-    cuts = [slots * i // (SEGMENTS * UNROLL) * UNROLL for i in range(SEGMENTS)] + [slots]
+    def segment(v, s):
+        cut = [slots * i // (SEGMENTS * UNROLL) * UNROLL for i in (s, s + 1)]
+        terms(v, cut[0], slots if s == SEGMENTS - 1 else cut[1])
+
+    first, rest = z_order[:1], z_order[1:]
+    spread(0, 0)
     gather_own(0)
+    spread(1, 0)
+    raw[...] = jnp.zeros_like(raw)
+    for row, ref in enumerate((left_index, right_index, source_block, target_block)):
+        raw[row : row + 1, 0:slots] = ref[...]
+    planned[...] = jnp.zeros_like(planned)
+    for row, value in enumerate(plan_terms(raw[...], live[0], psi0.shape[0])):
+        planned[row : row + 1, :] = value
+    plan_copy = pltpu.make_async_copy(planned, plan, plan_sem)
+    plan_copy.start()
     hist[0] = jnp.zeros(hist.shape[1:], f32)
-    gather_far(0)
+    gather_far(0, z_order)
     gather_own(1)
     gather_near(0)
+    gather_far(1, first)
     gather_end(0)
     for load in loads:
         load.wait()
-    beside0 = {1: gather_far, 3: gather_near}
-    for s in range(SEGMENTS):
-        terms(0, cuts[s], cuts[s + 1])
-        if s in beside0:
-            beside0[s](1)
+    plan_copy.wait()
+
+    segment(0, 0)
+    gather_far(1, rest[: len(rest) // 2])
+    segment(0, 1)
+    gather_far(1, rest[len(rest) // 2 :])
+    for s in range(2, SEGMENTS - 1):
+        segment(0, s)
+    gather_near(1)
+    segment(0, SEGMENTS - 1)
+    reduce_core(0)
     gather_end(1)
-    reduce_core(0)
-    beside1 = {0: reduce_near, 3: reduce_far}
-    for s in range(SEGMENTS):
-        terms(1, cuts[s], cuts[s + 1])
-        if s in beside1:
-            beside1[s](0)
+    segment(1, 0)
+    reduce_near(0)
+    for s in range(1, SEGMENTS - 1):
+        segment(1, s)
+    reduce_far(0, first)
+    segment(1, SEGMENTS - 1)
     reduce_core(1)
+    reduce_far(0, rest)
     reduce_near(1)
-    reduce_far(1)
+    reduce_far(1, z_order)
     reduce_end(0)
     reduce_end(1)
     for copy in sent:
@@ -237,7 +272,7 @@
     vectors, rows, width = wavefunction.shape
     nblocks = devices * rows // width
     slots = left_index.shape[0]
-    plan = plan_terms(left_index, right_index, source_block, target_block, live_count, nblocks)
+    lanes = pl.cdiv(slots, 128) * 128
     sems = pltpu.SemaphoreType.DMA
     bf16 = jnp.bfloat16
     f32 = jnp.float32
@@ -247,9 +282,12 @@
     return pl.pallas_call(
         functools.partial(kernel, far, near),
         out_shape=jax.ShapeDtypeStruct(wavefunction.shape, f32),
-        in_specs=[pl.BlockSpec(memory_space=pltpu.SMEM), vmem, hbm, hbm],
+        in_specs=[pl.BlockSpec(memory_space=pltpu.SMEM)] + [vmem] * 5 + [hbm] * 2,
         out_specs=vmem,
         scratch_shapes=[
+            pltpu.VMEM((8, lanes), jnp.int32),
+            pltpu.VMEM((8, lanes), jnp.int32),
+            pltpu.SMEM((8, lanes), jnp.int32),
             pltpu.VMEM(left_ops.shape, bf16),
             pltpu.VMEM(right_ops.shape, bf16),
             pltpu.VMEM((nblocks, width, width), bf16),
@@ -263,6 +301,7 @@
             pltpu.VMEM((2, far, rows, width), bf16),
             pltpu.VMEM((2, far, rows, width), bf16),
             sems((2,)),
+            sems,
             sems((2, 2, far, 2)),
             sems((2, 2, near, far, 2)),
             sems((2, 2, near, far, 2)),
@@ -275,7 +314,13 @@
             bytes_accessed=4 * left_ops.size,
             transcendentals=0,
         ),
-    )(plan, wavefunction, left_ops, right_ops)
+    )(
+        live_count,
+        *(x.reshape(1, slots) for x in (left_index, right_index, source_block, target_block)),
+        wavefunction,
+        left_ops,
+        right_ops,
+    )
 
 
 def solution(mesh):

time: 73.2 us -> 52.1 us (0.71)
  Pallas kernels: 68.3 us -> 49.6 us
  other arithmetic: 2.39 us -> 0 us
    pallas_call x1, Pallas kernels: 68.3 us -> 49.6 us  [per_device(): pl.pallas_call(functools.partial(kernel, far, near), out_shape=jax.ShapeD...]
where the time goes in v2:
time: 52.1 us; the launch traced here: 51.9 us
  Pallas kernels  49.6 us (95%)
  local copies, waits for them, and re-layouts  1.67 us (3%)
  between operations  0.66 us (1%)
    pallas_call x1, Pallas kernels, per_device(): pl.pallas_call(functools.partial(kernel, far, near), out_shape=jax.ShapeD...  49.6 us
    unnamed x1, local copies, waits for them, and re-layouts  1.67 us

profile of v2, /device:TPU:0, one launch (start us, length us, event | category | flops | bytes accessed | tf_op | source)
XLA Modules:
  0.0 51.9 jit_solution(17967851186478354835)
XLA Ops:
  0.7 49.6 %shard_map.82 = f32[2,128,256]{2,1,0:T(8,128)} custom-call(s32[1]{0:T(128)S(6)} %copy.10.live, s32[1,96]{1,0:T(1,128)} %bitcast.4, s32[1,96]{1,0:T(1,128)} %bitcast.5, s32[1,96]{1,0:T(1,128)} %bitcast.6, s32[1,96]{1,0:T(1,128)} %bitcast.7, bf16[2,128,256]{2,1,0:T(8,128)(2,1)} %wave.1, bf16[32,256,256]{2,1,0:T(8,128)(2,1)} %left_hbm.1, ...), custom_call_target="tpu_custom_call" | custom-call | flops 12884901888 | bytes 8388608 | tf_op jit(solution)/shard_map/pallas_call | solution.py:282
  50.3 1.7 %copy.11 = f32[2,128,256]{2,1,0:T(8,128)} copy(f32[2,128,256]{2,1,0:T(8,128)} %shard_map.82) | data formatting | bytes 524288

commit v3 on v2

--- a/solution.py
+++ b/solution.py
@@ -175,7 +175,7 @@
     def reduce_core(v):
         finish(v)
         for dy in list(range(1, near)) + [0]:
-            for dz in z_order + [0]:
+            for dz in z_order[::-1] + [0]:
                 a, b = shift(z, dz, far), shift(y, dy, near)
                 send_c[v, dy, dz] = partial(v, index_of(a, b, 1 - c)).astype(bf16)
                 send(send_c.at[v, dy, dz], recv_c.at[v, dy, dz], sem_pair(csem, 1, v, dy, dz), sibling)
@@ -186,7 +186,7 @@
         return partial(v, index_of(a, b, c)) + recv_c[v, dy, dz].astype(f32)
 
     def reduce_near(v):
-        for dz in z_order + [0]:
+        for dz in z_order[::-1] + [0]:
             for dy in range(1, near):
                 send_y[v, dy, dz] = core_sum(v, dy, dz).astype(bf16)
                 send(send_y.at[v, dy, dz], recv_y.at[v, dy, dz], sem_pair(ysem, 1, v, dy, dz), y_peer[dy])
@@ -199,7 +199,7 @@
         return total
 
     def reduce_far(v, order):
-        for dz in order:
+        for dz in order[::-1]:
             send_z[v, dz] = near_sum(v, dz).astype(bf16)
             send(send_z.at[v, dz], recv_z.at[v, dz], sem_pair(zsem, 1, v, dz), z_peer[dz])
 
@@ -250,10 +250,10 @@
     reduce_near(0)
     for s in range(1, SEGMENTS - 1):
         segment(1, s)
-    reduce_far(0, first)
+    reduce_far(0, z_order[-1:])
     segment(1, SEGMENTS - 1)
     reduce_core(1)
-    reduce_far(0, rest)
+    reduce_far(0, z_order[:-1])
     reduce_near(1)
     reduce_far(1, z_order)
     reduce_end(0)

time: 52.1 us -> 51.5 us (0.988)
  Pallas kernels: 49.6 us -> 49 us
    pallas_call x1, Pallas kernels: 49.6 us -> 49 us  [per_device(): pl.pallas_call(functools.partial(kernel, far, near), out_shape=jax.ShapeD...]
where the time goes in v3:
time: 51.5 us; the launch traced here: 51.4 us
  Pallas kernels  49 us (95%)
  local copies, waits for them, and re-layouts  1.67 us (3%)
  between operations  0.66 us (1%)
    pallas_call x1, Pallas kernels, per_device(): pl.pallas_call(functools.partial(kernel, far, near), out_shape=jax.ShapeD...  49 us
    unnamed x1, local copies, waits for them, and re-layouts  1.67 us

profile of v3, /device:TPU:0, one launch (start us, length us, event | category | flops | bytes accessed | tf_op | source)
XLA Modules:
  0.0 51.4 jit_solution(7691846398998771967)
XLA Ops:
  0.7 49.0 %shard_map.82 = f32[2,128,256]{2,1,0:T(8,128)} custom-call(s32[1]{0:T(128)S(6)} %copy.10.live, s32[1,96]{1,0:T(1,128)} %bitcast.4, s32[1,96]{1,0:T(1,128)} %bitcast.5, s32[1,96]{1,0:T(1,128)} %bitcast.6, s32[1,96]{1,0:T(1,128)} %bitcast.7, bf16[2,128,256]{2,1,0:T(8,128)(2,1)} %wave.1, bf16[32,256,256]{2,1,0:T(8,128)(2,1)} %left_hbm.1, ...), custom_call_target="tpu_custom_call" | custom-call | flops 12884901888 | bytes 8388608 | tf_op jit(solution)/shard_map/pallas_call | solution.py:282
  49.7 1.7 %copy.11 = f32[2,128,256]{2,1,0:T(8,128)} copy(f32[2,128,256]{2,1,0:T(8,128)} %shard_map.82) | data formatting | bytes 524288
